TPU v7x, 32 devices: a whole 2x2x4 slice. The times are simulated.
32 devices in a mesh: grp: 1, gx: 16 (over z, y, x), gy: 2 (over core).
Axes of the slice: x: 2, y: 2, z: 4, core: 2. Of those that a mesh axis runs over, the one named last changes fastest.
Arguments:
- voltages: bfloat16 [2, 64, 8, 256, 256], P(None, 'grp', None, 'gx', 'gy'), may hold values from -6 to 6
Outputs:
- visibility: float32 [2, 64, 512, 512], P(None, ('grp', 'gy'), 'gx')
All inputs are finite; a program needn't handle non-finite values.
Results may differ from a plain program's by a relative error of at most 0.0024.
Values may be sent and summed in bfloat16 or wider, within the bound.
A program may use at most 128 MiB of HBM per device.

v0:
```python
import functools
import math

import jax
import jax.numpy as jnp
import ml_dtypes
import numpy as np
from jax import lax
from jax.experimental import pallas as pl
from jax.experimental.pallas import tpu as pltpu
from jax.sharding import PartitionSpec as P

NA = 256
T_SIZE = 8
NB = 512


def dft_table(row_count, col_count, sign_factor, scale_factor, out_type):
    row_index = lax.iota(jnp.int32, row_count)[:, None]
    col_index = lax.iota(jnp.int32, col_count)[None, :]
    phase_index = row_index * col_index % NB
    angles = 2.0 * math.pi / NB * phase_index.astype(jnp.float32)
    return (
        (jnp.cos(angles) * scale_factor).astype(out_type),
        (sign_factor * jnp.sin(angles) * scale_factor).astype(out_type),
    )


def plain(voltages):
    high = lax.Precision.HIGHEST
    f32 = jnp.float32
    fwd_re, fwd_im = dft_table(NA, NB, -1.0, 1.0, jnp.bfloat16)
    inv_re, inv_im = dft_table(NB, NB, 1.0, 1.0 / NB, jnp.float32)
    out_re, out_im = dft_table(NB, NB, 1.0, 1.0 / (NB * T_SIZE * NA), jnp.float32)
    turned = lax.all_to_all(voltages, "gy", split_axis=1, concat_axis=4, tiled=True)
    stacks, channels, snapshots, x_rows, y_cols = turned.shape
    gx_size = lax.axis_size("gx")
    item_count = channels * snapshots // gx_size
    group_snaps = min(item_count, snapshots)
    group_count = item_count // group_snaps
    item_rows = turned.reshape(2, channels * snapshots, x_rows, y_cols)
    received = lax.all_to_all(item_rows, "gx", split_axis=1, concat_axis=2, tiled=True)
    received = received.reshape(2, group_count, group_snaps, NA, NA)
    beam_re = jnp.einsum(
        "gtxy,yv->gtxv", received[0], fwd_re, preferred_element_type=f32
    ) - jnp.einsum("gtxy,yv->gtxv", received[1], fwd_im, preferred_element_type=f32)
    beam_im = jnp.einsum(
        "gtxy,yv->gtxv", received[0], fwd_im, preferred_element_type=f32
    ) + jnp.einsum("gtxy,yv->gtxv", received[1], fwd_re, preferred_element_type=f32)
    beam_re = beam_re.astype(jnp.bfloat16)
    beam_im = beam_im.astype(jnp.bfloat16)
    full_re = jnp.einsum("gtxv,xu->gtuv", beam_re, fwd_re, preferred_element_type=f32) - jnp.einsum(
        "gtxv,xu->gtuv", beam_im, fwd_im, preferred_element_type=f32
    )
    full_im = jnp.einsum("gtxv,xu->gtuv", beam_re, fwd_im, preferred_element_type=f32) + jnp.einsum(
        "gtxv,xu->gtuv", beam_im, fwd_re, preferred_element_type=f32
    )
    power = jnp.sum(full_re * full_re + full_im * full_im, axis=1)
    per_channel = gx_size * group_count // channels
    lag_re = jnp.einsum("guv,ul->glv", power, inv_re, precision=high)
    lag_im = jnp.einsum("guv,ul->glv", power, inv_im, precision=high)
    partial_value = jnp.stack([lag_re, lag_im], axis=1)[None]
    gathered_lags = lax.all_to_all(partial_value, "gx", split_axis=3, concat_axis=0, tiled=True)
    lag_rows_dev = gathered_lags.shape[3]
    lag_sums = jnp.sum(gathered_lags.reshape(channels, per_channel, 2, lag_rows_dev, NB), axis=1)
    vis_re = jnp.einsum("clv,vm->clm", lag_sums[:, 0], out_re, precision=high) - jnp.einsum(
        "clv,vm->clm", lag_sums[:, 1], out_im, precision=high
    )
    vis_im = jnp.einsum("clv,vm->clm", lag_sums[:, 0], out_im, precision=high) + jnp.einsum(
        "clv,vm->clm", lag_sums[:, 1], out_re, precision=high
    )
    return jnp.stack([vis_re, vis_im])


HALF = NB // 2
MESH = pl.DeviceIdType.MESH
T_PART = 4
GROUP = 4


def pair_of(x):
    high = x.astype(ml_dtypes.bfloat16)
    return np.stack([high, (x - high.astype(np.float64)).astype(ml_dtypes.bfloat16)])


def fixed_tables():
    turn = 2.0 * np.pi / NB
    a, b = np.arange(NA), np.arange(HALF)
    cos = np.cos(turn * (np.outer(a, b) % NB))
    sin = np.sin(turn * (np.outer(a, b) % NB))
    alt = 1.0 - 2.0 * (np.arange(NB) % 2)
    sin[:, 0] = alt[:NA]
    first = np.concatenate([cos, sin], axis=1).astype(ml_dtypes.bfloat16)
    second = np.ascontiguousarray(first.T)
    lag = np.outer(np.arange(NB), b) % NB
    lag_cos = 2.0 * np.cos(turn * lag) / NB
    lag_cos[:, 0] = 1.0 / NB
    lag_sin = 4.0 * np.sin(turn * lag) / NB
    out_phase = lag.T
    out_sin = np.sin(turn * out_phase)
    out_sin[0] = alt
    out = np.concatenate([np.cos(turn * out_phase), out_sin]) / (NB * T_SIZE * NA)
    return first, second, pair_of(lag_cos), pair_of(lag_sin), pair_of(out)


def flip(value, mask, bits):
    out = 0
    for k in range(bits):
        unit = 2**k
        out = out + lax.rem(lax.div(value, unit) + lax.div(mask, unit), 2) * unit
    return out


def rest(x):
    return x - x.astype(jnp.bfloat16).astype(jnp.float32)


def kernel(gx_size, gy_size, v_ref, t1_ref, t2_ref, tc_ref, ts_ref, to_ref, out_ref, rv, t1, t2, tc, ts, to, even, odd, nyq,
           hbuf, hrecv, tab_sem, v_send, v_recv, h_send, h_recv):
    f32, bf16 = jnp.float32, jnp.bfloat16
    _, channels, snaps, x_rows, y_cols = v_ref.shape
    count = gx_size * gy_size
    bits = count.bit_length() - 1
    owned = channels // count
    lag_rows = NB // gx_size
    grp, gx, gy = lax.axis_index("grp"), lax.axis_index("gx"), lax.axis_index("gy")
    me = gx * gy_size + gy
    parts = snaps // T_PART

    tables = [
        pltpu.make_async_copy(src, dst, tab_sem.at[n])
        for n, (src, dst) in enumerate(((t1_ref, t1), (t2_ref, t2), (tc_ref, tc), (ts_ref, ts), (to_ref, to)))
    ]
    for copy in tables:
        copy.start()

    barrier = pltpu.get_barrier_semaphore()

    def greet(s, carry):
        other = flip(me, s, bits)
        pl.semaphore_signal(
            barrier, inc=1, device_id=(grp, lax.div(other, gy_size), lax.rem(other, gy_size)), device_id_type=MESH
        )
        return carry

    lax.fori_loop(1, count, greet, 0)
    pl.semaphore_wait(barrier, count - 1)

    x_at = pl.ds(pl.multiple_of(gx * x_rows, x_rows), x_rows)
    y_at = pl.ds(pl.multiple_of(gy * y_cols, y_cols), y_cols)

    for ch in range(owned):
        for part in range(parts):
            times = pl.ds(part * T_PART, T_PART)
            sem_at = ch * parts + part

            def send(n, carry):
                s = lax.rem(n, 2) * (count // 2) + lax.div(n, 2)
                other = flip(me, s, bits)
                pltpu.make_async_remote_copy(
                    src_ref=v_ref.at[:, other_channel(other), times],
                    dst_ref=rv.at[ch, :, times, x_at, y_at],
                    send_sem=v_send,
                    recv_sem=v_recv.at[sem_at],
                    device_id=(grp, lax.div(other, gy_size), lax.rem(other, gy_size)),
                    device_id_type=MESH,
                ).start()
                return carry

            def other_channel(other):
                ox, oy = lax.div(other, gy_size), lax.rem(other, gy_size)
                return oy * (channels // gy_size) + ox * owned + ch

            lax.fori_loop(1, count, send, 0)
            pltpu.make_async_copy(
                v_ref.at[:, other_channel(me), times], rv.at[ch, :, times, x_at, y_at], v_recv.at[sem_at]
            ).start()

    for copy in tables:
        copy.wait()

    lane0 = lax.broadcasted_iota(jnp.int32, (NA, HALF), 1) == 0
    row0 = lax.broadcasted_iota(jnp.int32, (HALF, HALF), 0) == 0
    dot = functools.partial(jnp.dot, preferred_element_type=f32)

    for ch in range(owned):
        even[...] = jnp.zeros_like(even)
        odd[...] = jnp.zeros_like(odd)
        nyq[...] = jnp.zeros_like(nyq)
        for part in range(parts):
            landed = rv.at[ch, :, pl.ds(part * T_PART, T_PART)]
            pltpu.make_async_copy(landed, landed, v_recv.at[ch * parts + part]).wait()

            def snapshot(t, carry):
                re = dot(rv[ch, 0, t], t1[...])
                im = dot(rv[ch, 1, t], t1[...])
                cr, sr, ci, si = re[:, :HALF], re[:, HALF:], im[:, :HALF], im[:, HALF:]
                halves = (
                    (cr + jnp.where(lane0, 0.0, si), ci - jnp.where(lane0, 0.0, sr)),
                    (jnp.where(lane0, sr, cr - si), jnp.where(lane0, si, ci + sr)),
                )
                for n, (b_re, b_im) in enumerate(halves):
                    at = slice(n * HALF, (n + 1) * HALF)
                    re = dot(t2[...], b_re.astype(bf16))
                    im = dot(t2[...], b_im.astype(bf16))
                    cr, sr, ci, si = re[:HALF], re[HALF:], im[:HALF], im[HALF:]
                    nyq[:, at] += sr[:8] * sr[:8] + si[:8] * si[:8]
                    sr, si = jnp.where(row0, 0.0, sr), jnp.where(row0, 0.0, si)
                    even[:, at] += (cr * cr + ci * ci) + (sr * sr + si * si)
                    odd[:, at] += cr * si - ci * sr
                return carry

            lax.fori_loop(part * T_PART, (part + 1) * T_PART, snapshot, 0)

        e_hi = even[...].astype(bf16)
        e_lo = (even[...] - e_hi.astype(f32)).astype(bf16)
        o_hi = odd[...].astype(bf16)
        o_lo = (odd[...] - o_hi.astype(f32)).astype(bf16)
        alt = 1.0 - 2.0 * lax.rem(lax.broadcasted_iota(jnp.int32, (HALF, 1), 0), 2).astype(f32)
        top = nyq[0:1, :] * (1.0 / NB)
        mask = lax.broadcasted_iota(jnp.int32, (HALF, HALF), 1) == 0
        for n in range(2):
            rows = slice(n * HALF, (n + 1) * HALF)
            h_re = dot(tc[0, rows], e_hi) + dot(tc[0, rows], e_lo) + dot(tc[1, rows], e_hi) + alt * top
            h_im = dot(ts[0, rows], o_hi) + dot(ts[0, rows], o_lo) + dot(ts[1, rows], o_hi)
            rp, rm, ip, im = h_re[:, :HALF], h_re[:, HALF:], h_im[:, :HALF], h_im[:, HALF:]
            slots = [
                jnp.where(mask, rp, rp + rm),
                jnp.where(mask, rm, im - ip),
                jnp.where(mask, ip, ip + im),
                jnp.where(mask, im, rp - rm),
            ]
            if n == 0:
                slots[1] = jnp.where(row0 & ~mask, rest(rp - rm), slots[1])
                slots[2] = jnp.where(row0, rest(slots[0]), slots[2])
                slots[3] = jnp.where(row0 & mask, rest(rm), slots[3])
            for k, slot in enumerate(slots):
                hbuf[ch, rows, k * HALF : (k + 1) * HALF] = slot.astype(bf16)

        def send_lags(n, carry):
            s = lax.rem(n, 2) * (gx_size // 2) + lax.div(n, 2)
            other = flip(gx, s, gx_size.bit_length() - 1)
            pltpu.make_async_remote_copy(
                src_ref=hbuf.at[ch, pl.ds(pl.multiple_of(other * lag_rows, lag_rows), lag_rows)],
                dst_ref=hrecv.at[ch, gx],
                send_sem=h_send.at[ch],
                recv_sem=h_recv.at[ch, lax.div(gx, GROUP)],
                device_id=(grp, other, gy),
                device_id_type=MESH,
            ).start()
            return carry

        lax.fori_loop(1, gx_size, send_lags, 0)
        pltpu.make_async_copy(
            hbuf.at[ch, pl.ds(pl.multiple_of(gx * lag_rows, lag_rows), lag_rows)], hrecv.at[ch, gx], h_recv.at[ch, lax.div(gx, GROUP)]
        ).start()

    own_group = lax.div(gx, GROUP)
    zero = jnp.zeros((gx_size, HALF), bf16)
    left = lax.broadcasted_iota(jnp.int32, (gx_size, HALF), 1) == 0

    for ch in range(owned):

        def finish(n, carry):
            group = flip(own_group, n, (gx_size // GROUP).bit_length() - 1)
            sources = pl.ds(group * GROUP, GROUP)
            landed = hrecv.at[ch, sources]
            pltpu.make_async_copy(landed, landed, h_recv.at[ch, group]).wait()
            for part in range(2):
                x = hrecv[ch, sources, :, part * NB : (part + 1) * NB].reshape(GROUP * lag_rows, NB)
                y = dot(x, to[0]) + dot(x, to[1])
                out_ref[part, sources, ch] = y.reshape(GROUP, lag_rows, NB)
            return carry

        lax.fori_loop(0, gx_size // GROUP, finish, 0)

        @pl.when(gx == 0)
        def _():
            row = hrecv[ch, :, 0, :]
            a_hi, s1, a_lo, s3 = (row[:, k * HALF : (k + 1) * HALF] for k in range(4))
            for part in range(2):
                total = 0.0
                for a, b in ((a_hi, s1), (a_lo, s3)):
                    x = [a, jnp.where(left, b, zero)] if part == 0 else [zero, jnp.where(left, zero, b)]
                    x = jnp.concatenate(x, axis=1)
                    total += dot(x, to[0]) + dot(x, to[1])
                out_ref[part, :, ch, 0, :] = total

    for ch in range(owned):
        sent = hbuf.at[ch, pl.ds(0, (gx_size - 1) * lag_rows)]
        pltpu.make_async_copy(sent, sent, h_send.at[ch]).wait()
    sent = v_ref.at[:, pl.ds(0, channels - owned)]
    pltpu.make_async_copy(sent, sent, v_send).wait()


def fused(gx_size, gy_size, voltages):
    _, channels, snaps, _, _ = voltages.shape
    owned = channels // (gx_size * gy_size)
    lag_rows = NB // gx_size
    tables = [jnp.asarray(table) for table in fixed_tables()]
    bf16, f32 = jnp.bfloat16, jnp.float32
    dma = pltpu.SemaphoreType.DMA
    out = pl.pallas_call(
        functools.partial(kernel, gx_size, gy_size),
        out_shape=pltpu.VMEM((2, gx_size, owned, lag_rows, NB), f32),
        in_specs=[pl.BlockSpec(memory_space=pltpu.HBM)] * 6,
        out_specs=pl.BlockSpec(memory_space=pltpu.VMEM),
        scratch_shapes=[
            pltpu.VMEM((owned, 2, snaps, NA, NA), bf16),
            *[pltpu.VMEM(table.shape, bf16) for table in tables],
            pltpu.VMEM((HALF, NB), f32),
            pltpu.VMEM((HALF, NB), f32),
            pltpu.VMEM((8, NB), f32),
            pltpu.VMEM((owned, NB, 2 * NB), bf16),
            pltpu.VMEM((owned, gx_size, lag_rows, 2 * NB), bf16),
            dma((5,)),
            dma,
            dma((owned * snaps // T_PART,)),
            dma((owned,)),
            dma((owned, gx_size // GROUP)),
        ],
        compiler_params=pltpu.CompilerParams(
            collective_id=0, has_side_effects=True, vmem_limit_bytes=40 * 2**20
        ),
        cost_estimate=pl.CostEstimate(flops=2 * 10**10, bytes_accessed=12 * 2**20, transcendentals=0),
    )(*[pltpu.with_memory_space_constraint(x, pltpu.HBM) for x in (voltages, *tables)])
    return out.reshape(2, gx_size * owned, lag_rows, NB)


def local(gx_size, gy_size, voltages):
    _, channels, snaps, x_rows, y_cols = voltages.shape
    count = gx_size * gy_size
    even_split = count & (count - 1) == 0 and gx_size >= 4 and gy_size >= 2 and channels % count == 0
    whole_tiles = x_rows % 16 == 0 and y_cols % 128 == 0 and (NB // gx_size) % 16 == 0 and snaps % T_PART == 0
    if even_split and whole_tiles:
        return fused(gx_size, gy_size, voltages)
    return plain(voltages)


def solution(mesh):
    return jax.shard_map(
        functools.partial(local, mesh.shape["gx"], mesh.shape["gy"]),
        mesh=mesh,
        in_specs=(P(None, "grp", None, "gx", "gy"),),
        out_specs=P(None, ("grp", "gy"), "gx", None),
        check_vma=False,
    )
```

profile of v0, /device:TPU:13, one launch (start us, length us, event | category | flops | bytes accessed | tf_op | source)
XLA Modules:
  0.0 144.1 jit_solution(1734138290580304660)
XLA Ops:
  0.0 142.1 %shard_map.64 = f32[2,16,2,32,512]{4,3,2,1,0:T(8,128)S(1)} custom-call(bf16[2,64,8,16,128]{4,3,2,1,0:T(8,128)(2,1)} %v_ref.1, bf16[256,512]{1,0:T(8,128)(2,1)} %constant.10.clone.t1_ref, bf16[512,256]{1,0:T(8,128)(2,1)} %constant.11.clone.t2_ref, bf16[2,512,256]{2,1,0:T(8,128)(2,1)} %constant.12.clone.tc_ref, bf16[2,512,256]{2,1,0:T(8,128)(2,1)} %constant.13.clone.ts_ref, ...), custom_call_target="tpu_custom_call" | custom-call | flops 20000000000 | bytes 12582912 | tf_op jit(solution)/shard_map/pallas_call | solution.py:303
  142.1 2.0 %copy.8 = f32[2,32,32,512]{3,2,1,0:T(8,128)} copy(f32[2,32,32,512]{3,2,1,0:T(8,128)S(1)} %bitcast.1) | data formatting | bytes 8388608
where the time goes:
time: 144 us
  Pallas kernels  142 us (99%)
  local copies, waits for them, and re-layouts  2.02 us (1%)
    pallas_call x1, Pallas kernels, fused(): pl.pallas_call(functools.partial(kernel, gx_size, gy_size), out_shape=plt...  142 us

commit v1 on v0

--- a/solution.py
+++ b/solution.py
@@ -116,7 +116,7 @@
 
 
 def kernel(gx_size, gy_size, v_ref, t1_ref, t2_ref, tc_ref, ts_ref, to_ref, out_ref, rv, t1, t2, tc, ts, to, even, odd, nyq,
-           hbuf, hrecv, tab_sem, v_send, v_recv, h_send, h_recv):
+           hbuf, hrecv, all_in, tab_sem, v_send, v_recv, h_send, h_recv):
     f32, bf16 = jnp.float32, jnp.bfloat16
     _, channels, snaps, x_rows, y_cols = v_ref.shape
     count = gx_size * gy_size
@@ -127,6 +127,42 @@
     me = gx * gy_size + gy
     parts = snaps // T_PART
 
+    barrier = pltpu.get_barrier_semaphore()
+    mirror_mask = gx_size * 3 // 4
+    mirror = flip(gx, mirror_mask, gx_size.bit_length() - 1)
+    pl.semaphore_signal(barrier, inc=1, device_id=(grp, mirror, 0), device_id_type=MESH)
+    for k in range(1, gx_size):
+        pl.semaphore_signal(barrier, inc=1, device_id=(grp, lax.rem(gx + k, gx_size), 1), device_id_type=MESH)
+
+    @pl.when(gy == 0)
+    def _():
+        pl.semaphore_signal(barrier, inc=1, device_id=(grp, gx, 1), device_id_type=MESH)
+
+    x_at = pl.ds(pl.multiple_of(gx * x_rows, x_rows), x_rows)
+    y_at = pl.ds(pl.multiple_of(gy * y_cols, y_cols), y_cols)
+
+    def channel_of(ox, oy, ch):
+        return oy * (channels // gy_size) + ox * owned + ch
+
+    def send_block(ox, oy, ch, part):
+        times = pl.ds(part * T_PART, T_PART)
+        pltpu.make_async_remote_copy(
+            src_ref=v_ref.at[:, channel_of(ox, oy, ch), times],
+            dst_ref=rv.at[ch, :, times, x_at, y_at],
+            send_sem=v_send,
+            recv_sem=v_recv.at[ch * parts + part],
+            device_id=(grp, ox, oy),
+            device_id_type=MESH,
+        ).start()
+
+    @pl.when(gy == 0)
+    def _():
+        pl.semaphore_wait(barrier, gy_size)
+        for ch in range(owned):
+            for part in range(parts):
+                for oy in range(gy_size):
+                    send_block(mirror, oy, ch, part)
+
     tables = [
         pltpu.make_async_copy(src, dst, tab_sem.at[n])
         for n, (src, dst) in enumerate(((t1_ref, t1), (t2_ref, t2), (tc_ref, tc), (ts_ref, ts), (to_ref, to)))
@@ -134,46 +170,32 @@
     for copy in tables:
         copy.start()
 
-    barrier = pltpu.get_barrier_semaphore()
-
-    def greet(s, carry):
-        other = flip(me, s, bits)
-        pl.semaphore_signal(
-            barrier, inc=1, device_id=(grp, lax.div(other, gy_size), lax.rem(other, gy_size)), device_id_type=MESH
-        )
-        return carry
-
-    lax.fori_loop(1, count, greet, 0)
-    pl.semaphore_wait(barrier, count - 1)
-
-    x_at = pl.ds(pl.multiple_of(gx * x_rows, x_rows), x_rows)
-    y_at = pl.ds(pl.multiple_of(gy * y_cols, y_cols), y_cols)
+    @pl.when(gy == 1)
+    def _():
+        pl.semaphore_wait(barrier, count - 1)
+        pl.semaphore_signal(all_in, inc=1, device_id=(grp, gx, 0), device_id_type=MESH)
+
+    @pl.when(gy == 0)
+    def _():
+        pl.semaphore_wait(all_in, 1)
 
     for ch in range(owned):
         for part in range(parts):
             times = pl.ds(part * T_PART, T_PART)
-            sem_at = ch * parts + part
 
             def send(n, carry):
                 s = lax.rem(n, 2) * (count // 2) + lax.div(n, 2)
                 other = flip(me, s, bits)
-                pltpu.make_async_remote_copy(
-                    src_ref=v_ref.at[:, other_channel(other), times],
-                    dst_ref=rv.at[ch, :, times, x_at, y_at],
-                    send_sem=v_send,
-                    recv_sem=v_recv.at[sem_at],
-                    device_id=(grp, lax.div(other, gy_size), lax.rem(other, gy_size)),
-                    device_id_type=MESH,
-                ).start()
+
+                @pl.when((gy == 1) | (lax.div(s, gy_size) != mirror_mask))
+                def _():
+                    send_block(lax.div(other, gy_size), lax.rem(other, gy_size), ch, part)
+
                 return carry
-
-            def other_channel(other):
-                ox, oy = lax.div(other, gy_size), lax.rem(other, gy_size)
-                return oy * (channels // gy_size) + ox * owned + ch
 
             lax.fori_loop(1, count, send, 0)
             pltpu.make_async_copy(
-                v_ref.at[:, other_channel(me), times], rv.at[ch, :, times, x_at, y_at], v_recv.at[sem_at]
+                v_ref.at[:, channel_of(gx, gy, ch), times], rv.at[ch, :, times, x_at, y_at], v_recv.at[ch * parts + part]
             ).start()
 
     for copy in tables:
@@ -313,6 +335,7 @@
             pltpu.VMEM((8, NB), f32),
             pltpu.VMEM((owned, NB, 2 * NB), bf16),
             pltpu.VMEM((owned, gx_size, lag_rows, 2 * NB), bf16),
+            pltpu.SemaphoreType.REGULAR,
             dma((5,)),
             dma,
             dma((owned * snaps // T_PART,)),
@@ -330,7 +353,7 @@
 def local(gx_size, gy_size, voltages):
     _, channels, snaps, x_rows, y_cols = voltages.shape
     count = gx_size * gy_size
-    even_split = count & (count - 1) == 0 and gx_size >= 4 and gy_size >= 2 and channels % count == 0
+    even_split = count & (count - 1) == 0 and gx_size >= 4 and gy_size == 2 and channels % count == 0
     whole_tiles = x_rows % 16 == 0 and y_cols % 128 == 0 and (NB // gx_size) % 16 == 0 and snaps % T_PART == 0
     if even_split and whole_tiles:
         return fused(gx_size, gy_size, voltages)

time: 144 us -> 143 us (level)
  Pallas kernels: 142 us -> 140 us
    pallas_call x1, Pallas kernels: 142 us -> 140 us  [fused(): pl.pallas_call(functools.partial(kernel, gx_size, gy_size), out_shape=plt...]
where the time goes in v1:
time: 143 us; the launch traced here: 142 us
  Pallas kernels  140 us (98%)
  local copies, waits for them, and re-layouts  2.02 us (1%)
    pallas_call x1, Pallas kernels, fused(): pl.pallas_call(functools.partial(kernel, gx_size, gy_size), out_shape=plt...  140 us

profile of v1, /device:TPU:13, one launch (start us, length us, event | category | flops | bytes accessed | tf_op | source)
XLA Modules:
  0.0 142.2 jit_solution(13105546450725903062)
XLA Ops:
  0.0 140.2 %shard_map.64 = f32[2,16,2,32,512]{4,3,2,1,0:T(8,128)S(1)} custom-call(bf16[2,64,8,16,128]{4,3,2,1,0:T(8,128)(2,1)} %v_ref.1, bf16[256,512]{1,0:T(8,128)(2,1)} %constant.10.clone.t1_ref, bf16[512,256]{1,0:T(8,128)(2,1)} %constant.11.clone.t2_ref, bf16[2,512,256]{2,1,0:T(8,128)(2,1)} %constant.12.clone.tc_ref, bf16[2,512,256]{2,1,0:T(8,128)(2,1)} %constant.13.clone.ts_ref, ...), custom_call_target="tpu_custom_call" | custom-call | flops 20000000000 | bytes 12582912 | tf_op jit(solution)/shard_map/pallas_call | solution.py:325
  140.2 2.0 %copy.8 = f32[2,32,32,512]{3,2,1,0:T(8,128)} copy(f32[2,32,32,512]{3,2,1,0:T(8,128)S(1)} %bitcast.1) | data formatting | bytes 8388608

commit v2 on v1

--- a/solution.py
+++ b/solution.py
@@ -128,15 +128,23 @@
     parts = snaps // T_PART
 
     barrier = pltpu.get_barrier_semaphore()
-    mirror_mask = gx_size * 3 // 4
-    mirror = flip(gx, mirror_mask, gx_size.bit_length() - 1)
-    pl.semaphore_signal(barrier, inc=1, device_id=(grp, mirror, 0), device_id_type=MESH)
-    for k in range(1, gx_size):
-        pl.semaphore_signal(barrier, inc=1, device_id=(grp, lax.rem(gx + k, gx_size), 1), device_id_type=MESH)
-
-    @pl.when(gy == 0)
+    quarter = gx_size // 4
+    gx_bits = gx_size.bit_length() - 1
+    mirror = flip(gx, 3 * quarter, gx_bits)
+    inner = lax.div(lax.rem(gx + quarter, gx_size), 2 * quarter) == 1
+
+    @pl.when(inner)
     def _():
-        pl.semaphore_signal(barrier, inc=1, device_id=(grp, gx, 1), device_id_type=MESH)
+        for oy in range(gy_size):
+            pl.semaphore_signal(barrier, inc=1, device_id=(grp, mirror, oy), device_id_type=MESH)
+
+    for k in range(2 * quarter):
+        outer = (3 * quarter + k) % gx_size
+        for oy in range(gy_size):
+
+            @pl.when((outer != gx) | (oy != gy))
+            def _():
+                pl.semaphore_signal(barrier, inc=1, device_id=(grp, outer, oy), device_id_type=MESH)
 
     x_at = pl.ds(pl.multiple_of(gx * x_rows, x_rows), x_rows)
     y_at = pl.ds(pl.multiple_of(gy * y_cols, y_cols), y_cols)
@@ -155,7 +163,7 @@
             device_id_type=MESH,
         ).start()
 
-    @pl.when(gy == 0)
+    @pl.when(inner)
     def _():
         pl.semaphore_wait(barrier, gy_size)
         for ch in range(owned):
@@ -170,14 +178,14 @@
     for copy in tables:
         copy.start()
 
-    @pl.when(gy == 1)
+    @pl.when(inner)
+    def _():
+        pl.semaphore_wait(all_in, 1)
+
+    @pl.when(~inner)
     def _():
         pl.semaphore_wait(barrier, count - 1)
-        pl.semaphore_signal(all_in, inc=1, device_id=(grp, gx, 0), device_id_type=MESH)
-
-    @pl.when(gy == 0)
-    def _():
-        pl.semaphore_wait(all_in, 1)
+        pl.semaphore_signal(all_in, inc=1, device_id=(grp, flip(gx, quarter, gx_bits), gy), device_id_type=MESH)
 
     for ch in range(owned):
         for part in range(parts):
@@ -187,7 +195,7 @@
                 s = lax.rem(n, 2) * (count // 2) + lax.div(n, 2)
                 other = flip(me, s, bits)
 
-                @pl.when((gy == 1) | (lax.div(s, gy_size) != mirror_mask))
+                @pl.when(~inner | (lax.div(s, gy_size) != 3 * quarter))
                 def _():
                     send_block(lax.div(other, gy_size), lax.rem(other, gy_size), ch, part)
 

time: 143 us -> 143 us (level)
  no operation moved by 1% of the time
where the time goes in v2:
time: 143 us; the launch traced here: 142 us
  Pallas kernels  140 us (98%)
  local copies, waits for them, and re-layouts  2.02 us (1%)
    pallas_call x1, Pallas kernels, fused(): pl.pallas_call(functools.partial(kernel, gx_size, gy_size), out_shape=plt...  140 us

profile of v2, /device:TPU:13, one launch (start us, length us, event | category | flops | bytes accessed | tf_op | source)
XLA Modules:
  0.0 141.5 jit_solution(9389348341099269665)
XLA Ops:
  0.0 139.5 %shard_map.64 = f32[2,16,2,32,512]{4,3,2,1,0:T(8,128)S(1)} custom-call(bf16[2,64,8,16,128]{4,3,2,1,0:T(8,128)(2,1)} %v_ref.1, bf16[256,512]{1,0:T(8,128)(2,1)} %constant.10.clone.t1_ref, bf16[512,256]{1,0:T(8,128)(2,1)} %constant.11.clone.t2_ref, bf16[2,512,256]{2,1,0:T(8,128)(2,1)} %constant.12.clone.tc_ref, bf16[2,512,256]{2,1,0:T(8,128)(2,1)} %constant.13.clone.ts_ref, ...), custom_call_target="tpu_custom_call" | custom-call | flops 20000000000 | bytes 12582912 | tf_op jit(solution)/shard_map/pallas_call | solution.py:333
  139.5 2.0 %copy.8 = f32[2,32,32,512]{3,2,1,0:T(8,128)} copy(f32[2,32,32,512]{3,2,1,0:T(8,128)S(1)} %bitcast.1) | data formatting | bytes 8388608

commit v3 on v2

--- a/solution.py
+++ b/solution.py
@@ -267,9 +267,7 @@
             for k, slot in enumerate(slots):
                 hbuf[ch, rows, k * HALF : (k + 1) * HALF] = slot.astype(bf16)
 
-        def send_lags(n, carry):
-            s = lax.rem(n, 2) * (gx_size // 2) + lax.div(n, 2)
-            other = flip(gx, s, gx_size.bit_length() - 1)
+        def send_lags_to(other):
             pltpu.make_async_remote_copy(
                 src_ref=hbuf.at[ch, pl.ds(pl.multiple_of(other * lag_rows, lag_rows), lag_rows)],
                 dst_ref=hrecv.at[ch, gx],
@@ -278,9 +276,20 @@
                 device_id=(grp, other, gy),
                 device_id_type=MESH,
             ).start()
+
+        def send_lags(n, carry):
+            row = max(quarter // 2, 1)
+            far = flip(gx, 2 * quarter + n, gx_bits)
+            far = far - lax.rem(far, quarter) + lax.div(lax.rem(n, quarter), row) * row + lax.rem(far, row)
+            send_lags_to(far)
+
+            @pl.when(n > 0)
+            def _():
+                send_lags_to(flip(gx, n, gx_bits))
+
             return carry
 
-        lax.fori_loop(1, gx_size, send_lags, 0)
+        lax.fori_loop(0, 2 * quarter, send_lags, 0)
         pltpu.make_async_copy(
             hbuf.at[ch, pl.ds(pl.multiple_of(gx * lag_rows, lag_rows), lag_rows)], hrecv.at[ch, gx], h_recv.at[ch, lax.div(gx, GROUP)]
         ).start()

time: 143 us -> 142 us (level)
  no operation moved by 1% of the time
where the time goes in v3:
time: 142 us
  Pallas kernels  140 us (99%)
  local copies, waits for them, and re-layouts  2.02 us (1%)
    pallas_call x1, Pallas kernels, fused(): pl.pallas_call(functools.partial(kernel, gx_size, gy_size), out_shape=plt...  140 us

profile of v3, /device:TPU:13, one launch (start us, length us, event | category | flops | bytes accessed | tf_op | source)
XLA Modules:
  0.0 141.7 jit_solution(7962179983429884011)
XLA Ops:
  0.0 139.6 %shard_map.64 = f32[2,16,2,32,512]{4,3,2,1,0:T(8,128)S(1)} custom-call(bf16[2,64,8,16,128]{4,3,2,1,0:T(8,128)(2,1)} %v_ref.1, bf16[256,512]{1,0:T(8,128)(2,1)} %constant.10.clone.t1_ref, bf16[512,256]{1,0:T(8,128)(2,1)} %constant.11.clone.t2_ref, bf16[2,512,256]{2,1,0:T(8,128)(2,1)} %constant.12.clone.tc_ref, bf16[2,512,256]{2,1,0:T(8,128)(2,1)} %constant.13.clone.ts_ref, ...), custom_call_target="tpu_custom_call" | custom-call | flops 20000000000 | bytes 12582912 | tf_op jit(solution)/shard_map/pallas_call | solution.py:342
  139.6 2.0 %copy.8 = f32[2,32,32,512]{3,2,1,0:T(8,128)} copy(f32[2,32,32,512]{3,2,1,0:T(8,128)S(1)} %bitcast.1) | data formatting | bytes 8388608

commit v4 on v3

--- a/solution.py
+++ b/solution.py
@@ -136,7 +136,11 @@
     @pl.when(inner)
     def _():
         for oy in range(gy_size):
-            pl.semaphore_signal(barrier, inc=1, device_id=(grp, mirror, oy), device_id_type=MESH)
+
+            @pl.when(oy <= gy)
+            def _():
+                pl.semaphore_signal(barrier, inc=1, device_id=(grp, mirror, oy), device_id_type=MESH)
+
 
     for k in range(2 * quarter):
         outer = (3 * quarter + k) % gx_size
@@ -165,11 +169,15 @@
 
     @pl.when(inner)
     def _():
-        pl.semaphore_wait(barrier, gy_size)
+        pl.semaphore_wait(barrier, gy_size - gy)
         for ch in range(owned):
             for part in range(parts):
                 for oy in range(gy_size):
-                    send_block(mirror, oy, ch, part)
+
+                    @pl.when(oy >= gy)
+                    def _():
+                        send_block(mirror, oy, ch, part)
+
 
     tables = [
         pltpu.make_async_copy(src, dst, tab_sem.at[n])
@@ -195,7 +203,7 @@
                 s = lax.rem(n, 2) * (count // 2) + lax.div(n, 2)
                 other = flip(me, s, bits)
 
-                @pl.when(~inner | (lax.div(s, gy_size) != 3 * quarter))
+                @pl.when(~inner | (lax.div(s, gy_size) != 3 * quarter) | (lax.rem(other, gy_size) < gy))
                 def _():
                     send_block(lax.div(other, gy_size), lax.rem(other, gy_size), ch, part)
 
@@ -280,7 +288,9 @@
         def send_lags(n, carry):
             row = max(quarter // 2, 1)
             far = flip(gx, 2 * quarter + n, gx_bits)
-            far = far - lax.rem(far, quarter) + lax.div(lax.rem(n, quarter), row) * row + lax.rem(far, row)
+            y, k = lax.div(lax.rem(n, quarter), row), lax.rem(n, row)
+            x = jnp.where((y == 0) | (lax.rem(gx, quarter) < row), lax.rem(far, row), k)
+            far = far - lax.rem(far, quarter) + y * row + x
             send_lags_to(far)
 
             @pl.when(n > 0)

time: 142 us -> 142 us (level)
  no operation moved by 1% of the time
where the time goes in v4:
time: 142 us; the launch traced here: 141 us
  Pallas kernels  139 us (98%)
  local copies, waits for them, and re-layouts  2.02 us (1%)
    pallas_call x1, Pallas kernels, fused(): pl.pallas_call(functools.partial(kernel, gx_size, gy_size), out_shape=plt...  139 us

profile of v4, /device:TPU:13, one launch (start us, length us, event | category | flops | bytes accessed | tf_op | source)
XLA Modules:
  0.0 141.4 jit_solution(8618479320989558586)
XLA Ops:
  0.0 139.4 %shard_map.64 = f32[2,16,2,32,512]{4,3,2,1,0:T(8,128)S(1)} custom-call(bf16[2,64,8,16,128]{4,3,2,1,0:T(8,128)(2,1)} %v_ref.1, bf16[256,512]{1,0:T(8,128)(2,1)} %constant.10.clone.t1_ref, bf16[512,256]{1,0:T(8,128)(2,1)} %constant.11.clone.t2_ref, bf16[2,512,256]{2,1,0:T(8,128)(2,1)} %constant.12.clone.tc_ref, bf16[2,512,256]{2,1,0:T(8,128)(2,1)} %constant.13.clone.ts_ref, ...), custom_call_target="tpu_custom_call" | custom-call | flops 20000000000 | bytes 12582912 | tf_op jit(solution)/shard_map/pallas_call | solution.py:352
  139.4 2.0 %copy.8 = f32[2,32,32,512]{3,2,1,0:T(8,128)} copy(f32[2,32,32,512]{3,2,1,0:T(8,128)S(1)} %bitcast.1) | data formatting | bytes 8388608

commit v5 on v4

--- a/solution.py
+++ b/solution.py
@@ -141,7 +141,6 @@
             def _():
                 pl.semaphore_signal(barrier, inc=1, device_id=(grp, mirror, oy), device_id_type=MESH)
 
-
     for k in range(2 * quarter):
         outer = (3 * quarter + k) % gx_size
         for oy in range(gy_size):
@@ -177,7 +176,6 @@
                     @pl.when(oy >= gy)
                     def _():
                         send_block(mirror, oy, ch, part)
-
 
     tables = [
         pltpu.make_async_copy(src, dst, tab_sem.at[n])
@@ -289,7 +287,7 @@
             row = max(quarter // 2, 1)
             far = flip(gx, 2 * quarter + n, gx_bits)
             y, k = lax.div(lax.rem(n, quarter), row), lax.rem(n, row)
-            x = jnp.where((y == 0) | (lax.rem(gx, quarter) < row), lax.rem(far, row), k)
+            x = jnp.where(lax.rem(gx, quarter) < row, lax.rem(far, row), k)
             far = far - lax.rem(far, quarter) + y * row + x
             send_lags_to(far)
 

time: 142 us -> 142 us (level)
  no operation moved by 1% of the time
where the time goes in v5:
time: 142 us; the launch traced here: 141 us
  Pallas kernels  139 us (98%)
  local copies, waits for them, and re-layouts  2.02 us (1%)
    pallas_call x1, Pallas kernels, fused(): pl.pallas_call(functools.partial(kernel, gx_size, gy_size), out_shape=plt...  139 us

profile of v5, /device:TPU:13, one launch (start us, length us, event | category | flops | bytes accessed | tf_op | source)
XLA Modules:
  0.0 141.4 jit_solution(1348170186605060078)
XLA Ops:
  0.0 139.4 %shard_map.64 = f32[2,16,2,32,512]{4,3,2,1,0:T(8,128)S(1)} custom-call(bf16[2,64,8,16,128]{4,3,2,1,0:T(8,128)(2,1)} %v_ref.1, bf16[256,512]{1,0:T(8,128)(2,1)} %constant.10.clone.t1_ref, bf16[512,256]{1,0:T(8,128)(2,1)} %constant.11.clone.t2_ref, bf16[2,512,256]{2,1,0:T(8,128)(2,1)} %constant.12.clone.tc_ref, bf16[2,512,256]{2,1,0:T(8,128)(2,1)} %constant.13.clone.ts_ref, ...), custom_call_target="tpu_custom_call" | custom-call | flops 20000000000 | bytes 12582912 | tf_op jit(solution)/shard_map/pallas_call | solution.py:350
  139.4 2.0 %copy.8 = f32[2,32,32,512]{3,2,1,0:T(8,128)} copy(f32[2,32,32,512]{3,2,1,0:T(8,128)S(1)} %bitcast.1) | data formatting | bytes 8388608

commit v6 on v4

--- a/solution.py
+++ b/solution.py
@@ -202,8 +202,12 @@
             def send(n, carry):
                 s = lax.rem(n, 2) * (count // 2) + lax.div(n, 2)
                 other = flip(me, s, bits)
-
-                @pl.when(~inner | (lax.div(s, gy_size) != 3 * quarter) | (lax.rem(other, gy_size) < gy))
+                half_col = quarter * gy_size // 2
+                m = lax.rem(lax.div(n, 2), quarter * gy_size)
+                fixed = other - lax.rem(other, quarter * gy_size) + lax.div(m, half_col) * half_col + lax.rem(other, half_col)
+                other = jnp.where(lax.rem(n, 2) == 1, fixed, other)
+
+                @pl.when(~inner | (lax.div(other, gy_size) != mirror) | (lax.rem(other, gy_size) < gy))
                 def _():
                     send_block(lax.div(other, gy_size), lax.rem(other, gy_size), ch, part)
 

time: 142 us -> 141 us (level)
  no operation moved by 1% of the time
where the time goes in v6:
time: 141 us
  Pallas kernels  139 us (99%)
  local copies, waits for them, and re-layouts  2.02 us (1%)
    pallas_call x1, Pallas kernels, fused(): pl.pallas_call(functools.partial(kernel, gx_size, gy_size), out_shape=plt...  139 us

profile of v6, /device:TPU:13, one launch (start us, length us, event | category | flops | bytes accessed | tf_op | source)
XLA Modules:
  0.0 141.3 jit_solution(3706829235548649321)
XLA Ops:
  0.0 139.3 %shard_map.64 = f32[2,16,2,32,512]{4,3,2,1,0:T(8,128)S(1)} custom-call(bf16[2,64,8,16,128]{4,3,2,1,0:T(8,128)(2,1)} %v_ref.1, bf16[256,512]{1,0:T(8,128)(2,1)} %constant.10.clone.t1_ref, bf16[512,256]{1,0:T(8,128)(2,1)} %constant.11.clone.t2_ref, bf16[2,512,256]{2,1,0:T(8,128)(2,1)} %constant.12.clone.tc_ref, bf16[2,512,256]{2,1,0:T(8,128)(2,1)} %constant.13.clone.ts_ref, ...), custom_call_target="tpu_custom_call" | custom-call | flops 20000000000 | bytes 12582912 | tf_op jit(solution)/shard_map/pallas_call | solution.py:356
  139.3 2.0 %copy.8 = f32[2,32,32,512]{3,2,1,0:T(8,128)} copy(f32[2,32,32,512]{3,2,1,0:T(8,128)S(1)} %bitcast.1) | data formatting | bytes 8388608

commit v7 on v4

--- a/solution.py
+++ b/solution.py
@@ -200,7 +200,10 @@
             times = pl.ds(part * T_PART, T_PART)
 
             def send(n, carry):
-                s = lax.rem(n, 2) * (count // 2) + lax.div(n, 2)
+                k = lax.div(n, 2)
+                block = quarter * gy_size
+                k = jnp.where(lax.rem(n, 2) == 1, lax.rem(k, 2) * block + lax.div(k, 2), k)
+                s = lax.rem(n, 2) * (count // 2) + k
                 other = flip(me, s, bits)
 
                 @pl.when(~inner | (lax.div(s, gy_size) != 3 * quarter) | (lax.rem(other, gy_size) < gy))

time: 142 us -> 141 us (level)
  no operation moved by 1% of the time
where the time goes in v7:
time: 141 us
  Pallas kernels  139 us (99%)
  local copies, waits for them, and re-layouts  2.02 us (1%)
    pallas_call x1, Pallas kernels, fused(): pl.pallas_call(functools.partial(kernel, gx_size, gy_size), out_shape=plt...  139 us

profile of v7, /device:TPU:13, one launch (start us, length us, event | category | flops | bytes accessed | tf_op | source)
XLA Modules:
  0.0 141.3 jit_solution(2895960210488440602)
XLA Ops:
  0.0 139.3 %shard_map.64 = f32[2,16,2,32,512]{4,3,2,1,0:T(8,128)S(1)} custom-call(bf16[2,64,8,16,128]{4,3,2,1,0:T(8,128)(2,1)} %v_ref.1, bf16[256,512]{1,0:T(8,128)(2,1)} %constant.10.clone.t1_ref, bf16[512,256]{1,0:T(8,128)(2,1)} %constant.11.clone.t2_ref, bf16[2,512,256]{2,1,0:T(8,128)(2,1)} %constant.12.clone.tc_ref, bf16[2,512,256]{2,1,0:T(8,128)(2,1)} %constant.13.clone.ts_ref, ...), custom_call_target="tpu_custom_call" | custom-call | flops 20000000000 | bytes 12582912 | tf_op jit(solution)/shard_map/pallas_call | solution.py:355
  139.3 2.0 %copy.8 = f32[2,32,32,512]{3,2,1,0:T(8,128)} copy(f32[2,32,32,512]{3,2,1,0:T(8,128)S(1)} %bitcast.1) | data formatting | bytes 8388608
